TPU v7x, 768 devices: a whole 4x8x12 slice. The times are simulated.
768 devices in a mesh: grp: 12 (over z), own: 64 (over y, x, core).
Axes of the slice: x: 4, y: 8, z: 12, core: 2. Of those that a mesh axis runs over, the one named last changes fastest.
Arguments:
- upstream: bfloat16 [3072, 64, 4, 512], P(('grp', 'own')), may hold values from -6 to 6
- pooled: bfloat16 [3072, 64, 960], P(('grp', 'own')), may hold values from -6 to 6
- projection: bfloat16 [960, 512], replicated, may hold values from -0.5 to 0.5
- embedding: float32 [196608, 960], P(('grp', 'own')), may hold values from -4 to 4
- row_state: float32 [4, 196608], P(None, ('grp', 'own')), may hold values from 0.01 to 1
- lookups: int32 [768, 4, 256, 16], P(('grp', 'own')), may hold values from 0 to 255
- bag_sizes: int32 [768, 4, 256], P(('grp', 'own')), may hold values from 1 to 16, as said below
Outputs:
- updated_rows: float32 [196608, 960], P(('grp', 'own'))
- updated_state: float32 [4, 196608], P(None, ('grp', 'own'))
- proj_grad: float32 [960, 512], replicated
Inputs may be any that keep to these rules, and one draw needn't show every extreme that they name: `bag_sizes`: positions at or past a bag's size are not looked up.
All inputs are finite; a program needn't handle non-finite values.
Results may differ from a plain program's by a relative error of at most 0.00051.
Values may be sent and summed in bfloat16 or wider, within the bound.
A program may use at most 32 MiB of HBM per device.

v0:
```python
import math

import jax
import jax.numpy as jnp
from jax import lax
from jax.sharding import PartitionSpec as P

DIM_A = 64
DIM_B = 128
DIM_C = 256
DIM_D = 512
BAG = 16


LEARN = 0.05


def column_blocks():
    blocks = []
    offset = 0
    for breadth in (DIM_A, DIM_B, DIM_C, DIM_D):
        blocks.append((offset, breadth))
        offset += breadth
    return blocks


def narrowed(grads, projection):
    pieces = []
    for member, (offset, breadth) in enumerate(column_blocks()):
        pieces.append(
            jnp.einsum(
                "...e,ke->...k",
                grads[..., member, :],
                projection[offset : offset + breadth],
                preferred_element_type=jnp.float32,
            )
        )
    return jnp.concatenate(pieces, axis=-1).astype(jnp.bfloat16)


def on_device(upstream, pooled, projection, embedding, row_state, lookups, bag_sizes):
    arrived = lax.all_to_all(upstream, "own", split_axis=1, concat_axis=0, tiled=True)
    bag_grad = narrowed(arrived[:, 0], projection)
    terms = []
    for member, (offset, breadth) in enumerate(column_blocks()):
        terms.append(
            jnp.einsum(
                "sok,soe->ke",
                pooled[:, :, offset : offset + breadth],
                upstream[:, :, member, :],
                preferred_element_type=jnp.float32,
            )
        )
    local_term = jnp.concatenate(terms, axis=0)
    summed = lax.psum(local_term, ("grp", "own"))
    total_bags = upstream.shape[0] * lax.axis_size("grp") * lax.axis_size("own") * upstream.shape[1]
    proj_grad = summed * (1.0 / math.sqrt(total_bags))
    rows_here = embedding.shape[0]
    group_size = bag_grad.shape[0]
    positions = lax.broadcasted_iota(jnp.int32, (group_size, BAG), 1)
    row_ids = lax.broadcasted_iota(jnp.int32, (rows_here, 1, 1), 0)
    new_rows = []
    new_state = []
    for member, (offset, breadth) in enumerate(column_blocks()):
        valid = positions < bag_sizes[0, member][:, None]
        matched = (lookups[0, member][None, :, :] == row_ids) & valid[None, :, :]
        tallies = jnp.sum(jnp.where(matched, 1.0, 0.0), axis=2).astype(jnp.bfloat16)
        grad = jnp.dot(
            tallies, bag_grad[:, offset : offset + breadth], preferred_element_type=jnp.float32
        )
        state = row_state[member] + jnp.mean(grad * grad, axis=1)
        new_state.append(state)
        new_rows.append(
            embedding[:, offset : offset + breadth] - LEARN * grad / jnp.sqrt(state)[:, None]
        )
    updated_rows = jnp.concatenate(new_rows, axis=1)
    updated_state = jnp.stack(new_state, axis=0)
    return (updated_rows, updated_state, proj_grad)


def solution(mesh):
    return jax.shard_map(
        on_device,
        mesh=mesh,
        in_specs=(
            P(("grp", "own"), None, None, None),
            P(("grp", "own"), None, None),
            P(),
            P(("grp", "own"), None),
            P(None, ("grp", "own")),
            P(("grp", "own"), None, None, None),
            P(("grp", "own"), None, None),
        ),
        out_specs=(P(("grp", "own"), None), P(None, ("grp", "own")), P()),
        check_vma=False,
    )
```

profile of v0, /device:TPU:1, one launch (start us, length us, event | category | flops | bytes accessed | tf_op | source)
XLA Modules:
  0.0 533.1 jit_solution(7135163175089604211)
XLA Ops:
  7.2 2.9 copy.54
  10.0 14.6 %all-to-all-start = ((bf16[4,64,4,512]{3,2,0,1:T(4,128)(2,1)}), bf16[4,64,4,512]{3,2,0,1:T(4,128)(2,1)S(1)}, u32[]{:S(2)}, u32[]{:S(2)}) async-start(bf16[4,64,4,512]{3,2,0,1:T(4,128)(2,1)} %copy.54), calls=%async_computation | async-start | bytes 2097152 | tf_op jit(solution)/shard_map/all_to_all | solution.py:42
  24.6 0.0 copy-start.2
  24.7 0.0 all-reduce.2.cloned.1.call-start
  24.7 1.6 fusion.40
  26.3 0.2 convolution_bitcast_fusion.3
  26.5 0.3 convolution_bitcast_fusion.2
  26.8 0.3 convolution_bitcast_fusion.1
  27.1 0.5 convolution_bitcast_fusion
  27.6 1.4 pad_maximum_fusion
  29.0 0.0 all-reduce.2.cloned.1.call-update
  29.0 0.7 copy-done.6
  29.7 0.3 slice-done
  30.0 0.2 copy.69
  30.3 3.8 select_reduce_fusion.2
  34.1 3.2 select_reduce_fusion
  37.2 473.6 %all-reduce.2.cloned.1.call-done = f32[960,512]{1,0:T(8,128)} async-done(((f32[960,512]{1,0:T(8,128)}), f32[960,512]{1,0:T(8,128)}) %all-reduce.2.cloned.1.call-update) | async-done | bytes 1966096 | tf_op jit(solution)/shard_map/psum | solution.py:55
  510.9 3.0 broadcast_multiply_fusion
  513.9 0.0 all-to-all-done
  513.9 2.5 fusion.41
  516.4 2.2 multiply_reduce_fusion.3
  518.6 1.5 multiply_reduce_fusion.2
  520.1 1.5 multiply_reduce_fusion.1
  521.6 1.7 multiply_reduce_fusion
  523.4 0.1 copy.58
  523.6 0.1 copy.57
  523.7 0.0 copy-done.4
  523.7 0.1 copy.56
  523.8 0.1 divide_subtract_fusion
  523.9 0.4 pad_maximum_fusion.1
  524.4 1.3 copy.64
  525.6 0.6 pad_maximum_fusion.2
  (32 shorter events, 0.2 us)
Async XLA Ops:
  7.2 17.5 %copy-start = (bf16[4,64,4,512]{3,2,1,0:T(4,128)(2,1)S(1)}, bf16[4,64,4,512]{3,2,1,0:T(4,128)(2,1)}, u32[]{:S(2)}) copy-start(bf16[4,64,4,512]{3,2,1,0:T(4,128)(2,1)} %param.7) | copy-start | bytes 3145732
  10.0 503.9 %all-to-all-start = ((bf16[4,64,4,512]{3,2,0,1:T(4,128)(2,1)}), bf16[4,64,4,512]{3,2,0,1:T(4,128)(2,1)S(1)}, u32[]{:S(2)}, u32[]{:S(2)}) async-start(bf16[4,64,4,512]{3,2,0,1:T(4,128)(2,1)} %copy.54), calls=%async_computation | async-start | bytes 2097152 | tf_op jit(solution)/shard_map/all_to_all | solution.py:42
  24.6 1.6 copy-start.2
  24.7 486.2 %all-reduce.2.cloned.1.call-start = ((), (), s32[]{:S(2)}) async-start(), calls=%async_computation.1 | async-start | bytes 3932160 | tf_op jit(solution)/shard_map/psum | solution.py:55
  29.0 0.7 copy-start.6
  29.0 1.1 slice-start
  29.0 1.3 copy-start.5
  516.4 5.2 copy-start.3
  516.4 6.9 %copy-start.7 = (f32[4,256]{1,0:T(4,128)S(1)}, f32[4,256]{1,0:T(4,128)}, u32[]{:S(2)}) copy-start(f32[4,256]{1,0:T(4,128)} %param.11) | copy-start | bytes 12292
  516.4 7.0 %copy-start.1 = (f32[256,960]{0,1:T(8,128)S(1)}, f32[256,960]{0,1:T(8,128)}, u32[]{:S(2)}) copy-start(f32[256,960]{0,1:T(8,128)} %param.10) | copy-start | bytes 2949124
  521.6 2.1 copy-start.4
Sparse Core Ops, SparseCore 0:
  31.4 479.3 all-reduce.1
where the time goes:
time: 533 us
  waiting for transfers between devices  474 us (89%)
  starting transfers between devices  14.6 us (3%)
  between operations  14.3 us (3%)
  other arithmetic  12.8 us (2%)
  local copies, waits for them, and re-layouts  9.65 us (2%)
  matrix products  8.08 us (2%)
    psum x1, waiting for transfers between devices, on_device(): summed = lax.psum(local_term, ('grp', 'own'))  474 us
    all_to_all x1, starting transfers between devices, on_device(): lax.all_to_all(upstream, 'own', split_axis=1, concat_axis=0, tiled=True)  14.6 us
  transfers between devices with their start and end apart: 2, of which 1 were waited for; matrix products, arithmetic and copies ran while one was open for 3% of the time, Pallas kernels for 0%

commit v1 on v0

v1 whole, which is shorter than its diff:
```python
import functools
import math

import jax
import jax.numpy as jnp
from jax import lax
from jax.experimental import pallas as pl
from jax.experimental.pallas import tpu as pltpu
from jax.sharding import PartitionSpec as P

BAG = 16
GB = 256
LEARN = 0.05
NX, NY, NZ = 4, 8, 12
N_OWN = 64
MESH = pl.DeviceIdType.MESH
F32 = jnp.float32
BF16 = jnp.bfloat16
CLASSES = ((0, 64), (64, 128), (192, 256), (448, 512))
BLOCKS = ((0, 1), (1, 1), (2, 2), (4, 4))


def kernel(
    ua, ub, uc, ud, pooled, proj, emb, state, looks, sizes,
    rows_out, state_out, pg_out,
    ua_v, ub_v, uc_v, ud_v, pooled_v, proj_v, emb_v, state_v, looks_v, sizes_v,
    acc, sib, xs, xr, ys, yr, z1, z2, pg,
    stage, abuf, arecv, tal, rows_v, state_new,
    in_sem, sib_s, sib_r, x_s, x_r, y_s, y_r, z1_s, z1_r, z2_s, z2_r,
    a_s, a_r, gy_s, gy_r, gx_s, gx_r, gs_s, gs_r, out_sem,
):
    g = lax.axis_index("grp")
    p = lax.axis_index("own")
    core = lax.rem(p, 2)
    xi = lax.rem(p // 2, NX)
    yi = p // (2 * NX)
    zq = g // 4
    zi = lax.rem(g, 4)
    other = 1 - core

    def at(y, x, c):
        return (g, (y * NX + x) * 2 + c)

    def remote(src, dst, send, recv, dev):
        return pltpu.make_async_remote_copy(
            src_ref=src, dst_ref=dst, send_sem=send, recv_sem=recv,
            device_id=dev, device_id_type=MESH,
        )

    ins = (
        (ua, ua_v), (ub, ub_v), (uc, uc_v), (ud, ud_v), (pooled, pooled_v),
        (proj, proj_v), (looks, looks_v), (sizes, sizes_v), (emb, emb_v), (state, state_v),
    )
    loads = [pltpu.make_async_copy(a, b, in_sem.at[i]) for i, (a, b) in enumerate(ins)]
    for load in loads:
        load.start()

    barrier = pltpu.get_barrier_semaphore()

    @pl.loop(1, N_OWN)
    def _(i):
        pl.semaphore_signal(barrier, inc=1, device_id=(g, lax.rem(p + i, N_OWN)), device_id_type=MESH)

    def z_near(i):
        return (zq * 4 + lax.rem(zi + i, 4), p)

    def z_far(i):
        return (lax.rem(g + 4 * i, NZ), p)

    for i in (1, 2, 3):
        pl.semaphore_signal(barrier, inc=1, device_id=z_near(i), device_id_type=MESH)
    for i in (1, 2):
        pl.semaphore_signal(barrier, inc=1, device_id=z_far(i), device_id_type=MESH)

    for load in loads[:5]:
        load.wait()

    def term(lo, hi, u):
        return lax.dot_general(
            pooled_v[:, lo:hi], u[...], (((0,), (0,)), ((), ())), preferred_element_type=F32
        )

    acc[0] = term(384, 960, ud_v)[64:576]
    acc[1, 0:128] = term(0, 128, ua_v)
    acc[1, 128:256] = term(0, 256, ub_v)[64:192]
    acc[1, 256:512] = term(128, 512, uc_v)[64:320]

    pl.semaphore_wait(barrier, N_OWN - 1 + 5)

    sib_dev = at(yi, xi, other)
    sib_copies = []
    for i in (2, 1, 3, 0):
        t = lax.rem(xi + i, NX)
        rows = pl.ds(pl.multiple_of(t * 128, 128), 128)
        copy = remote(acc.at[other, rows], sib.at[rows], sib_s.at[i], sib_r.at[i], sib_dev)
        copy.start()
        sib_copies.append((i, rows, t, copy))

    x_copies = []
    for i, rows, t, copy in sib_copies:
        copy.wait_recv()
        if i == 0:
            break
        xs[i - 1] = acc[core, rows] + sib[rows]
        out = remote(xs.at[i - 1], xr.at[i - 1], x_s.at[i - 1], x_r.at[i - 1], at(yi, t, core))
        out.start()
        x_copies.append(out)
    own_rows = sib_copies[3][1]

    loads[5].wait()
    for u, (offset, width), (block, number) in zip((ua_v, ub_v, uc_v, ud_v), CLASSES, BLOCKS):
        bag = lax.dot_general(
            u[...], proj_v[offset : offset + number * 128], (((1,), (1,)), ((), ())),
            preferred_element_type=F32,
        )
        for k in range(number):
            for s in range(4):
                stage[pl.ds(s * 8 + block + k, N_OWN, stride=32), :] = bag[
                    s * 64 : s * 64 + 64, k * 128 : k * 128 + 128
                ]
    abuf[...] = stage[...].reshape(N_OWN, 32, 128).astype(BF16)

    loads[6].wait()
    loads[7].wait()
    spread = lax.broadcasted_iota(jnp.int32, (GB, GB), 0)
    order = (spread & 63) * 4 + (spread >> 6)
    picked = jnp.where(order == lax.broadcasted_iota(jnp.int32, (GB, GB), 1), 1.0, 0.0).astype(BF16)
    for member in range(4):
        valid = lax.broadcasted_iota(jnp.int32, (BAG, GB), 0) < sizes_v[member : member + 1, :]
        wanted = jnp.where(valid, looks_v[member], -1)
        parts = []
        for r in range(0, GB, 64):
            ids = lax.broadcasted_iota(jnp.int32, (64, GB), 0) + r
            count = jnp.zeros((64, GB), F32)
            for l in range(BAG):
                count += jnp.where(wanted[l : l + 1, :] == ids, 1.0, 0.0)
            parts.append(count.astype(BF16))
        counts = jnp.concatenate(parts, axis=0)
        tal[member] = lax.dot_general(
            picked, counts, (((1,), (1,)), ((), ())), preferred_element_type=F32
        ).astype(BF16)

    total = acc[core, own_rows] + sib[own_rows]
    for i, copy in zip((2, 1, 3), x_copies):
        copy.wait_recv()
        total += xr[i - 1]
    for y in range(NY):
        ys[y] = total[y * 16 : y * 16 + 16]

    y_copies = []
    for i in (4, 3, 5, 2, 6, 1, 7):
        t = lax.rem(yi + i, NY)
        copy = remote(ys.at[t], yr.at[i - 1], y_s.at[i - 1], y_r.at[i - 1], at(t, xi, core))
        copy.start()
        y_copies.append((i, copy))

    def to_owner(i):
        t = lax.rem(p + i, N_OWN)
        return remote(abuf.at[t], arecv.at[p], a_s, a_r, (g, t))

    @pl.loop(1, N_OWN)
    def _(i):
        to_owner(i).start()

    arecv[p] = abuf[p]

    part = ys[yi]
    for i, copy in y_copies:
        copy.wait_recv()
        part += yr[i - 1]

    z1[zi] = part
    z1_copies = []
    for i in (1, 2, 3):
        copy = remote(z1.at[zi], z1.at[zi], z1_s.at[i - 1], z1_r.at[i - 1], z_near(i))
        copy.start()
        z1_copies.append(copy)
    for copy in z1_copies:
        copy.wait_recv()
    z2[zq] = (z1[0] + z1[1]) + (z1[2] + z1[3])
    z2_copies = []
    for i in (1, 2):
        copy = remote(z2.at[zq], z2.at[zq], z2_s.at[i - 1], z2_r.at[i - 1], z_far(i))
        copy.start()
        z2_copies.append(copy)
    for copy in z2_copies:
        copy.wait_recv()
    first = core * 32
    mine = first + xi * 8 + yi
    pg[mine] = (z2[0] + z2[1]) + z2[2]

    gy_copies = []
    for i in (4, 3, 5, 2, 6, 1, 7):
        t = lax.rem(yi + i, NY)
        copy = remote(pg.at[mine], pg.at[mine], gy_s.at[i - 1], gy_r.at[i - 1], at(t, xi, core))
        copy.start()
        gy_copies.append(copy)

    pltpu.make_async_copy(arecv.at[pl.ds(0, N_OWN - 1)], arecv.at[pl.ds(0, N_OWN - 1)], a_r).wait()
    loads[8].wait()
    loads[9].wait()
    stage[...] = arecv[...].astype(F32).reshape(N_OWN * 32, 128)
    for member, ((offset, width), (block, number)) in enumerate(zip(CLASSES, BLOCKS)):
        columns = []
        for k in range(number):
            columns.append(
                jnp.concatenate(
                    [stage[pl.ds(s * 8 + block + k, N_OWN, stride=32), :] for s in range(4)], axis=0
                ).astype(BF16)
            )
        bags = columns[0] if number == 1 else jnp.concatenate(columns, axis=1)
        grad = lax.dot_general(
            bags, tal[member], (((0,), (0,)), ((), ())), preferred_element_type=F32
        )[:width]
        new = state_v[member : member + 1, :] + jnp.sum(grad * grad, axis=0, keepdims=True) * (1.0 / width)
        state_new[member : member + 1, :] = new
        rows_v[offset : offset + width, :] = emb_v[offset : offset + width, :] - grad * (LEARN / jnp.sqrt(new))
    outs = [
        pltpu.make_async_copy(rows_v, rows_out, out_sem.at[0]),
        pltpu.make_async_copy(state_new, state_out, out_sem.at[1]),
    ]
    for out in outs:
        out.start()

    for copy in gy_copies:
        copy.wait_recv()

    def chunk(t):
        return pg.at[pl.ds(first + t * 8, 8)]

    gx_copies = []
    for i in (2, 1, 3):
        t = lax.rem(xi + i, NX)
        copy = remote(chunk(xi), chunk(xi), gx_s.at[i - 1], gx_r.at[i - 1], at(yi, t, core))
        copy.start()
        gx_copies.append((i, copy))
    gs_copies = [remote(chunk(xi), chunk(xi), gs_s.at[0], gs_r.at[0], sib_dev)]
    gs_copies[0].start()
    for i, copy in sorted(gx_copies, key=lambda pair: pair[0] % 2 == 0):
        copy.wait_recv()
        t = lax.rem(xi - i + NX, NX)
        hand = remote(chunk(t), chunk(t), gs_s.at[i], gs_r.at[i], sib_dev)
        hand.start()
        gs_copies.append(hand)
    for hand in gs_copies:
        hand.wait_recv()
    for i, (src, dst, number) in enumerate(((0, 28, 32), (32, 0, 4), (40, 4, 24))):
        out = pltpu.make_async_copy(
            pg.at[pl.ds(src, number)], pg_out.at[pl.ds(dst, number)], out_sem.at[2 + i]
        )
        out.start()
        outs.append(out)

    for group in ([c[3] for c in sib_copies], x_copies, [c for _, c in y_copies], z1_copies, z2_copies,
                  gy_copies, [c for _, c in gx_copies], gs_copies):
        for copy in group:
            copy.wait_send()

    @pl.loop(1, N_OWN)
    def _(i):
        to_owner(i).wait_send()

    for out in outs:
        out.wait()


def on_device(upstream, pooled, projection, embedding, row_state, lookups, bag_sizes):
    ups = [upstream[:, :, c, :].reshape(GB, 512) for c in range(4)]
    operands = (
        *ups, pooled.reshape(GB, 960), projection, embedding.T, row_state,
        jnp.transpose(lookups[0], (0, 2, 1)), bag_sizes[0],
    )
    dma = pltpu.SemaphoreType.DMA
    any_space = pl.BlockSpec(memory_space=pl.ANY)
    scratch = [pltpu.VMEM(a.shape, a.dtype) for a in operands] + [
        pltpu.VMEM((2, 512, 512), F32),
        pltpu.VMEM((512, 512), F32),
        pltpu.VMEM((3, 128, 512), F32),
        pltpu.VMEM((3, 128, 512), F32),
        pltpu.VMEM((8, 16, 512), F32),
        pltpu.VMEM((7, 16, 512), F32),
        pltpu.VMEM((4, 16, 512), F32),
        pltpu.VMEM((3, 16, 512), F32),
        pltpu.VMEM((64, 16, 512), F32),
        pltpu.VMEM((N_OWN * 32, 128), F32),
        pltpu.VMEM((N_OWN, 32, 128), BF16),
        pltpu.VMEM((N_OWN, 32, 128), BF16),
        pltpu.VMEM((4, GB, GB), BF16),
        pltpu.VMEM((960, GB), F32),
        pltpu.VMEM((4, GB), F32),
        dma((10,)),
        dma((4,)), dma((4,)), dma((3,)), dma((3,)), dma((7,)), dma((7,)),
        dma((3,)), dma((3,)), dma((2,)), dma((2,)),
        dma, dma, dma((7,)), dma((7,)), dma((3,)), dma((3,)), dma((4,)), dma((4,)), dma((5,)),
    ]
    rows_t, new_state, pg = pl.pallas_call(
        kernel,
        out_shape=(
            jax.ShapeDtypeStruct((960, GB), F32),
            jax.ShapeDtypeStruct((4, GB), F32),
            jax.ShapeDtypeStruct((60, 16, 512), F32),
        ),
        in_specs=[any_space] * len(operands),
        out_specs=(any_space,) * 3,
        scratch_shapes=scratch,
        compiler_params=pltpu.CompilerParams(
            collective_id=0, has_side_effects=True, vmem_limit_bytes=40 * 2**20
        ),
        name="fused",
    )(*operands)
    total_bags = upstream.shape[0] * lax.axis_size("grp") * lax.axis_size("own") * upstream.shape[1]
    return rows_t.T, new_state, pg.reshape(960, 512) * (1.0 / math.sqrt(total_bags))


def solution(mesh):
    return jax.shard_map(
        on_device,
        mesh=mesh,
        in_specs=(
            P(("grp", "own"), None, None, None),
            P(("grp", "own"), None, None),
            P(),
            P(("grp", "own"), None),
            P(None, ("grp", "own")),
            P(("grp", "own"), None, None, None),
            P(("grp", "own"), None, None),
        ),
        out_specs=(P(("grp", "own"), None), P(None, ("grp", "own")), P()),
        check_vma=False,
    )
```

time: 533 us -> 86.3 us (0.16)
  waiting for transfers between devices: 474 us -> 0 us
  Pallas kernels: 0 us -> 76.1 us
  starting transfers between devices: 14.6 us -> 0 us
  between operations: 14.3 us -> 0.73 us
  other arithmetic: 12.8 us -> 1.53 us
  matrix products: 8.08 us -> 0 us
    psum x1 -> x0, waiting for transfers between devices: 474 us -> none  [on_device(): summed = lax.psum(local_term, ('grp', 'own'))]
    pallas_call x0 -> x1, Pallas kernels: none -> 76.1 us  [on_device(): pl.pallas_call(kernel, out_shape=(jax.ShapeDtypeStruct((960, GB), F32), j...]
    all_to_all x1 -> x0, starting transfers between devices: 14.6 us -> none  [on_device(): lax.all_to_all(upstream, 'own', split_axis=1, concat_axis=0, tiled=True)]
    dot_general x8 -> x0, matrix products: 8.08 us -> none  [the longest x4 6.84 us: on_device(): jnp.dot(tallies, bag_grad[:, offset:offset + breadth], preferred_element_...]
    reduce_sum x2 -> x0, other arithmetic: 6.97 us -> none  [on_device(): tallies = jnp.sum(jnp.where(matched, 1.0, 0.0), axis=2).astype(jnp.bfloat16)]
  transfers between devices with their start and end apart: 2 -> 0, of which waited for: 1 -> 0; matrix products, arithmetic and copies ran while one was open for 3% -> 0% of each run, Pallas kernels for 0% -> 0%
where the time goes in v1:
time: 86.3 us; the launch traced here: 86.1 us
  Pallas kernels  76.1 us (88%)
  local copies, waits for them, and re-layouts  7.73 us (9%)
  other arithmetic  1.53 us (2%)
    pallas_call x1, Pallas kernels, on_device(): pl.pallas_call(kernel, out_shape=(jax.ShapeDtypeStruct((960, GB), F32), j...  76.1 us
    slice x1, local copies, waits for them, and re-layouts, on_device(): ups = [upstream[:, :, c, :].reshape(GB, 512) for c in range(4)]  4.63 us
    unnamed x18, local copies, waits for them, and re-layouts  3.1 us

profile of v1, /device:TPU:1, one launch (start us, length us, event | category | flops | bytes accessed | tf_op | source)
XLA Modules:
  0.0 86.1 jit_solution(16849774709280752426)
XLA Ops:
  0.6 4.6 %fusion = (bf16[4,64,1,512]{3,2,1,0:T(2,128)(2,1)S(1)}, bf16[4,64,1,512]{3,2,1,0:T(2,128)(2,1)S(1)}, bf16[4,64,1,512]{3,2,1,0:T(2,128)(2,1)S(1)}, bf16[4,64,1,512]{3,2,1,0:T(2,128)(2,1)S(1)}) fusion(bf16[4,64,4,512]{3,2,1,0:T(4,128)(2,1)} %param.7), kind=kLoop, calls=%fused_computation.1 | loop fusion | bytes 2097152 | tf_op jit(solution)/shard_map/slice | solution.py:268
  5.3 0.0 copy-start
  5.3 0.0 copy-start.1
  5.3 0.0 copy-start.2
  5.3 0.0 copy-start.3
  5.3 0.0 copy-start.4
  5.3 0.0 copy-start.5
  5.5 0.9 %copy-done = bf16[960,512]{1,0:T(8,128)(2,1)S(1)} copy-done((bf16[960,512]{1,0:T(8,128)(2,1)S(1)}, bf16[960,512]{1,0:T(8,128)(2,1)}, u32[]{:S(2)}) %copy-start) | copy-done | bytes 983064
  6.5 0.3 copy-done.1
  6.8 0.1 copy-done.2
  6.9 0.0 copy-done.3
  6.9 0.0 copy-done.4
  6.9 0.0 copy-done.5
  6.9 76.1 %fused.1 = (f32[960,256]{1,0:T(8,128)S(1)}, f32[4,256]{1,0:T(4,128)S(1)}, f32[60,16,512]{2,1,0:T(8,128)S(1)}) custom-call(bf16[256,512]{1,0:T(8,128)(2,1)S(1)} %bitcast.15, bf16[256,512]{1,0:T(8,128)(2,1)S(1)} %bitcast.14, bf16[256,512]{1,0:T(8,128)(2,1)S(1)} %bitcast.13, bf16[256,512]{1,0:T(8,128)(2,1)S(1)} %bitcast.12, bf16[256,960]{1,0:T(8,128)(2,1)S(1)} %bitcast.18, ...), custom_call_target="tpu_custom_call" | custom-call | tf_op jit(solution)/shard_map/fused/pallas_call | solution.py:296
  83.0 1.5 %broadcast_multiply_fusion = f32[60,16,512]{2,1,0:T(8,128)} fusion(f32[60,16,512]{2,1,0:T(8,128)S(1)} %get-tuple-element.8), kind=kLoop, calls=%fused_computation | loop fusion | flops 491520 | bytes 3932160 | tf_op jit(solution)/shard_map/mul | solution.py:312
  84.6 0.9 %copy.20 = f32[256,960]{0,1:T(8,128)} copy(f32[256,960]{0,1:T(8,128)S(1)} %bitcast.17) | data formatting | bytes 1966080
  85.5 0.6 copy.21
  (4 shorter events, 0.2 us)
Async XLA Ops:
  5.3 1.2 %copy-start = (bf16[960,512]{1,0:T(8,128)(2,1)S(1)}, bf16[960,512]{1,0:T(8,128)(2,1)}, u32[]{:S(2)}) copy-start(bf16[960,512]{1,0:T(8,128)(2,1)} %proj.1) | copy-start | bytes 2949124
  5.3 1.5 %copy-start.1 = (f32[256,960]{0,1:T(8,128)S(1)}, f32[256,960]{0,1:T(8,128)}, u32[]{:S(2)}) copy-start(f32[256,960]{0,1:T(8,128)} %param.10) | copy-start | bytes 2949124
  5.3 1.6 %copy-start.2 = (bf16[4,64,960]{2,1,0:T(8,128)(2,1)S(1)}, bf16[4,64,960]{2,1,0:T(8,128)(2,1)}, u32[]{:S(2)}) copy-start(bf16[4,64,960]{2,1,0:T(8,128)(2,1)} %param.8) | copy-start | bytes 1474564
  5.3 1.6 %copy-start.3 = (s32[1,4,256,16]{2,3,1,0:T(8,128)S(1)}, s32[1,4,256,16]{2,3,1,0:T(8,128)}, u32[]{:S(2)}) copy-start(s32[1,4,256,16]{2,3,1,0:T(8,128)} %param.12) | copy-start | bytes 196612
  5.3 1.6 %copy-start.4 = (f32[4,256]{1,0:T(4,128)S(1)}, f32[4,256]{1,0:T(4,128)}, u32[]{:S(2)}) copy-start(f32[4,256]{1,0:T(4,128)} %state.1) | copy-start | bytes 12292
  5.3 1.6 %copy-start.5 = (s32[1,4,256]{2,1,0:T(4,128)S(1)}, s32[1,4,256]{2,1,0:T(4,128)}, u32[]{:S(2)}) copy-start(s32[1,4,256]{2,1,0:T(4,128)} %param.13) | copy-start | bytes 12292

commit v2 on v1

--- a/solution.py
+++ b/solution.py
@@ -21,11 +21,12 @@
 
 
 def kernel(
-    ua, ub, uc, ud, pooled, proj, emb, state, looks, sizes,
+    scale,
+    ups, pooled, proj, emb, state, looks, sizes,
     rows_out, state_out, pg_out,
-    ua_v, ub_v, uc_v, ud_v, pooled_v, proj_v, emb_v, state_v, looks_v, sizes_v,
+    ups_v, pooled_v, proj_v, emb_v, state_v, looks_v, sizes_v,
     acc, sib, xs, xr, ys, yr, z1, z2, pg,
-    stage, abuf, arecv, tal, rows_v, state_new,
+    wide, uc_v, stage, abuf, arecv, tal, rows_v, state_new,
     in_sem, sib_s, sib_r, x_s, x_r, y_s, y_r, z1_s, z1_r, z2_s, z2_r,
     a_s, a_r, gy_s, gy_r, gx_s, gx_r, gs_s, gs_r, out_sem,
 ):
@@ -48,8 +49,7 @@
         )
 
     ins = (
-        (ua, ua_v), (ub, ub_v), (uc, uc_v), (ud, ud_v), (pooled, pooled_v),
-        (proj, proj_v), (looks, looks_v), (sizes, sizes_v), (emb, emb_v), (state, state_v),
+        (ups, ups_v), (pooled, pooled_v), (proj, proj_v), (looks, looks_v), (sizes, sizes_v), (emb, emb_v), (state, state_v),
     )
     loads = [pltpu.make_async_copy(a, b, in_sem.at[i]) for i, (a, b) in enumerate(ins)]
     for load in loads:
@@ -72,18 +72,30 @@
     for i in (1, 2):
         pl.semaphore_signal(barrier, inc=1, device_id=z_far(i), device_id_type=MESH)
 
-    for load in loads[:5]:
+    for load in loads[:1]:
         load.wait()
 
-    def term(lo, hi, u):
+    @pl.loop(0, 8)
+    def _(b):
+        some = ups_v[pl.ds(b * 32, 32)].astype(F32)
+        for t in range(4):
+            wide[t, pl.ds(pl.multiple_of(b * 128, 128), 128), :] = some[:, :, t * 128 : t * 128 + 128].reshape(128, 128)
+
+    for c in range(4):
+        for t in range(4):
+            uc_v[c, :, t * 128 : t * 128 + 128] = wide[t, pl.ds(c, GB, stride=4), :].astype(BF16)
+
+    loads[1].wait()
+
+    def term(lo, hi, c):
         return lax.dot_general(
-            pooled_v[:, lo:hi], u[...], (((0,), (0,)), ((), ())), preferred_element_type=F32
+            pooled_v[:, lo:hi], uc_v[c], (((0,), (0,)), ((), ())), preferred_element_type=F32
         )
 
-    acc[0] = term(384, 960, ud_v)[64:576]
-    acc[1, 0:128] = term(0, 128, ua_v)
-    acc[1, 128:256] = term(0, 256, ub_v)[64:192]
-    acc[1, 256:512] = term(128, 512, uc_v)[64:320]
+    acc[0] = term(384, 960, 3)[64:576]
+    acc[1, 0:128] = term(0, 128, 0)
+    acc[1, 128:256] = term(0, 256, 1)[64:192]
+    acc[1, 256:512] = term(128, 512, 2)[64:320]
 
     pl.semaphore_wait(barrier, N_OWN - 1 + 5)
 
@@ -107,10 +119,10 @@
         x_copies.append(out)
     own_rows = sib_copies[3][1]
 
-    loads[5].wait()
-    for u, (offset, width), (block, number) in zip((ua_v, ub_v, uc_v, ud_v), CLASSES, BLOCKS):
+    loads[2].wait()
+    for c, ((offset, width), (block, number)) in enumerate(zip(CLASSES, BLOCKS)):
         bag = lax.dot_general(
-            u[...], proj_v[offset : offset + number * 128], (((1,), (1,)), ((), ())),
+            uc_v[c], proj_v[offset : offset + number * 128], (((1,), (1,)), ((), ())),
             preferred_element_type=F32,
         )
         for k in range(number):
@@ -120,8 +132,8 @@
                 ]
     abuf[...] = stage[...].reshape(N_OWN, 32, 128).astype(BF16)
 
-    loads[6].wait()
-    loads[7].wait()
+    loads[3].wait()
+    loads[4].wait()
     spread = lax.broadcasted_iota(jnp.int32, (GB, GB), 0)
     order = (spread & 63) * 4 + (spread >> 6)
     picked = jnp.where(order == lax.broadcasted_iota(jnp.int32, (GB, GB), 1), 1.0, 0.0).astype(BF16)
@@ -187,7 +199,7 @@
         copy.wait_recv()
     first = core * 32
     mine = first + xi * 8 + yi
-    pg[mine] = (z2[0] + z2[1]) + z2[2]
+    pg[mine] = ((z2[0] + z2[1]) + z2[2]) * scale
 
     gy_copies = []
     for i in (4, 3, 5, 2, 6, 1, 7):
@@ -197,8 +209,8 @@
         gy_copies.append(copy)
 
     pltpu.make_async_copy(arecv.at[pl.ds(0, N_OWN - 1)], arecv.at[pl.ds(0, N_OWN - 1)], a_r).wait()
-    loads[8].wait()
-    loads[9].wait()
+    loads[5].wait()
+    loads[6].wait()
     stage[...] = arecv[...].astype(F32).reshape(N_OWN * 32, 128)
     for member, ((offset, width), (block, number)) in enumerate(zip(CLASSES, BLOCKS)):
         columns = []
@@ -264,10 +276,20 @@
         out.wait()
 
 
+def flush(rows, state, pg, rows_out, state_out, pg_out, sem):
+    pairs = ((pg, pg_out), (rows, rows_out), (state, state_out))
+    copies = [pltpu.make_async_copy(a, b, sem.at[i]) for i, (a, b) in enumerate(pairs)]
+    for copy in copies:
+        copy.start()
+    for copy in copies:
+        copy.wait()
+
+
 def on_device(upstream, pooled, projection, embedding, row_state, lookups, bag_sizes):
-    ups = [upstream[:, :, c, :].reshape(GB, 512) for c in range(4)]
+    total_bags = upstream.shape[0] * lax.axis_size("grp") * lax.axis_size("own") * upstream.shape[1]
+    scale = 1.0 / math.sqrt(total_bags)
     operands = (
-        *ups, pooled.reshape(GB, 960), projection, embedding.T, row_state,
+        upstream.reshape(GB, 4, 512), pooled.reshape(GB, 960), projection, embedding.T, row_state,
         jnp.transpose(lookups[0], (0, 2, 1)), bag_sizes[0],
     )
     dma = pltpu.SemaphoreType.DMA
@@ -282,34 +304,44 @@
         pltpu.VMEM((4, 16, 512), F32),
         pltpu.VMEM((3, 16, 512), F32),
         pltpu.VMEM((64, 16, 512), F32),
+        pltpu.VMEM((4, 4 * GB, 128), F32),
+        pltpu.VMEM((4, GB, 512), BF16),
         pltpu.VMEM((N_OWN * 32, 128), F32),
         pltpu.VMEM((N_OWN, 32, 128), BF16),
         pltpu.VMEM((N_OWN, 32, 128), BF16),
         pltpu.VMEM((4, GB, GB), BF16),
         pltpu.VMEM((960, GB), F32),
         pltpu.VMEM((4, GB), F32),
-        dma((10,)),
+        dma((7,)),
         dma((4,)), dma((4,)), dma((3,)), dma((3,)), dma((7,)), dma((7,)),
         dma((3,)), dma((3,)), dma((2,)), dma((2,)),
         dma, dma, dma((7,)), dma((7,)), dma((3,)), dma((3,)), dma((4,)), dma((4,)), dma((5,)),
     ]
     rows_t, new_state, pg = pl.pallas_call(
-        kernel,
+        functools.partial(kernel, scale),
         out_shape=(
-            jax.ShapeDtypeStruct((960, GB), F32),
-            jax.ShapeDtypeStruct((4, GB), F32),
-            jax.ShapeDtypeStruct((60, 16, 512), F32),
+            pltpu.VMEM((960, GB), F32),
+            pltpu.VMEM((4, GB), F32),
+            pltpu.VMEM((60, 16, 512), F32),
         ),
-        in_specs=[any_space] * len(operands),
+        in_specs=[pl.BlockSpec(memory_space=pltpu.HBM)] * len(operands),
         out_specs=(any_space,) * 3,
         scratch_shapes=scratch,
         compiler_params=pltpu.CompilerParams(
-            collective_id=0, has_side_effects=True, vmem_limit_bytes=40 * 2**20
+            collective_id=0, has_side_effects=True, vmem_limit_bytes=54 * 2**20
         ),
         name="fused",
     )(*operands)
-    total_bags = upstream.shape[0] * lax.axis_size("grp") * lax.axis_size("own") * upstream.shape[1]
-    return rows_t.T, new_state, pg.reshape(960, 512) * (1.0 / math.sqrt(total_bags))
+    outs = (rows_t, new_state, pg)
+    rows_t, new_state, pg = pl.pallas_call(
+        flush,
+        out_shape=tuple(jax.ShapeDtypeStruct(a.shape, a.dtype) for a in outs),
+        in_specs=[any_space] * 3,
+        out_specs=(any_space,) * 3,
+        scratch_shapes=[dma((3,))],
+        name="flush",
+    )(*outs)
+    return rows_t.T, new_state, pg.reshape(960, 512)
 
 
 def solution(mesh):

time: 86.3 us -> 169 us (1.96)
  Pallas kernels: 76.1 us -> 166 us
  local copies, waits for them, and re-layouts: 7.73 us -> 2.84 us
    pallas_call x1 -> x2, Pallas kernels: 76.1 us -> 166 us  [the longest x1 90.6 us: on_device(): pl.pallas_call(flush, out_shape=tuple((jax.ShapeDtypeStruct(a.shape, a.dt...]
    slice x1 -> x0, local copies, waits for them, and re-layouts: 4.63 us -> none  [on_device(): ups = [upstream[:, :, c, :].reshape(GB, 512) for c in range(4)]]
where the time goes in v2:
time: 169 us
  Pallas kernels  166 us (98%)
  local copies, waits for them, and re-layouts  2.84 us (2%)
    pallas_call x1, Pallas kernels, on_device(): pl.pallas_call(flush, out_shape=tuple((jax.ShapeDtypeStruct(a.shape, a.dt...  90.6 us
    pallas_call x1, Pallas kernels, on_device(): pl.pallas_call(functools.partial(kernel, scale), out_shape=(pltpu.VMEM((9...  75.3 us

profile of v2, /device:TPU:1, one launch (start us, length us, event | category | flops | bytes accessed | tf_op | source)
XLA Modules:
  0.0 169.3 jit_solution(15596308483696702597)
XLA Ops:
  0.6 75.3 %fused.1 = (f32[960,256]{1,0:T(8,128)S(1)}, f32[4,256]{1,0:T(4,128)S(1)}, f32[60,16,512]{2,1,0:T(8,128)S(1)}) custom-call(bf16[256,4,512]{2,1,0:T(4,128)(2,1)} %bitcast.9, bf16[256,960]{1,0:T(8,128)(2,1)} %bitcast.11, bf16[960,512]{1,0:T(8,128)(2,1)} %proj.1, f32[960,256]{1,0:T(8,128)} %bitcast.10, f32[4,256]{1,0:T(4,128)} %state.1, s32[4,16,256]{2,1,0:T(8,128)} %bitcast.12, ...), custom_call_target="tpu_custom_call" | custom-call | tf_op jit(solution)/shard_map/fused/pallas_call | solution.py:320
  75.9 0.0 copy-start
  75.9 1.3 copy-done
  77.2 0.0 copy-start.1
  77.2 1.0 copy-done.1
  78.2 0.0 copy-start.2
  78.2 0.6 copy-done.2
  78.8 90.6 %flush.1 = (f32[960,256]{1,0:T(8,128)}, f32[4,256]{1,0:T(4,128)}, f32[60,16,512]{2,1,0:T(8,128)}) custom-call(f32[960,256]{1,0:T(8,128)} %copy-done.1, f32[4,256]{1,0:T(4,128)} %copy-done.2, f32[60,16,512]{2,1,0:T(8,128)} %copy-done), custom_call_target="tpu_custom_call" | custom-call | tf_op jit(solution)/shard_map/flush/pallas_call | solution.py:336
Async XLA Ops:
  75.9 1.3 copy-start
  77.2 1.0 copy-start.1
  78.2 0.6 copy-start.2

commit v3 on v2

v3 whole, which is shorter than its diff:
```python
import functools
import math

import jax
import jax.numpy as jnp
from jax import lax
from jax.experimental import pallas as pl
from jax.experimental.pallas import tpu as pltpu
from jax.sharding import PartitionSpec as P

BAG = 16
GB = 256
LEARN = 0.05
NX, NY, NZ = 4, 8, 12
N_OWN = 64
MESH = pl.DeviceIdType.MESH
F32 = jnp.float32
BF16 = jnp.bfloat16
CLASSES = ((0, 64), (64, 128), (192, 256), (448, 512))
BLOCKS = ((0, 1), (1, 1), (2, 2), (4, 4))


I16 = jnp.int16
X_ORDER = (2, 1, 3)
Y_ORDER = (4, 3, 5, 2, 6, 1, 7)
BOTH = (("y", 4), ("y", 3), ("x", 2), ("y", 5), ("y", 2), ("x", 1), ("y", 6), ("y", 1), ("x", 3), ("y", 7))


def pack(tiles, q):
    top = jnp.abs(tiles[0])
    for tile in tiles[1:]:
        top = jnp.maximum(top, jnp.abs(tile))
    power = jnp.ceil(jnp.log2(jnp.maximum(top, 1e-30) * 1.001))
    scale = jnp.exp2(15.0 - power)
    for k, tile in enumerate(tiles):
        q[k] = jnp.round(tile * scale).astype(jnp.int32).astype(I16)
    q[len(tiles)] = power.astype(jnp.int32).astype(I16)


def unpack(q, number):
    scale = jnp.exp2(q[number].astype(jnp.int32).astype(F32) - 15.0)
    return [q[k].astype(jnp.int32).astype(F32) * scale for k in range(number)]


def tiles_of(value):
    return [
        value[r : r + 16, c : c + 128]
        for r in range(0, value.shape[0], 16)
        for c in range(0, value.shape[1], 128)
    ]


def kernel(
    scale,
    ups, pooled, proj, emb, state, looks, sizes,
    rows_out, state_out, pg_out,
    ups_v, pooled_v, proj_v, emb_v, state_v, looks_v, sizes_v,
    acc, sib, x1s, x1r, y1s, y1r, y2s, y2r, x2s, x2r, z1, z2, ga, gb, gx, gy,
    wide, uc_v, stage, abuf, arecv, tal,
    in_sem, sib_s, sib_r, x1_s, x1_r, y1_s, y1_r, y2_s, y2_r, x2_s, x2_r, z1_s, z1_r, z2_s, z2_r,
    a_s, a_r, ga_s, ga_r, gb_s, gb_r, gx_s, gx_r, gy_s, gy_r, hx_s, hx_r, hy_s, hy_r,
):
    g = lax.axis_index("grp")
    p = lax.axis_index("own")
    core = lax.rem(p, 2)
    xi = lax.rem(p // 2, NX)
    yi = p // (2 * NX)
    zq = g // 4
    zi = lax.rem(g, 4)
    other = 1 - core

    def at(y, x, c):
        return (g, (y * NX + x) * 2 + c)

    def remote(src, dst, send, recv, dev):
        return pltpu.make_async_remote_copy(
            src_ref=src, dst_ref=dst, send_sem=send, recv_sem=recv,
            device_id=dev, device_id_type=MESH,
        )

    ins = (
        (ups, ups_v), (pooled, pooled_v), (proj, proj_v), (looks, looks_v), (sizes, sizes_v), (emb, emb_v), (state, state_v),
    )
    loads = [pltpu.make_async_copy(a, b, in_sem.at[i]) for i, (a, b) in enumerate(ins)]
    for load in loads:
        load.start()

    barrier = pltpu.get_barrier_semaphore()

    @pl.loop(1, N_OWN)
    def _(i):
        pl.semaphore_signal(barrier, inc=1, device_id=(g, lax.rem(p + i, N_OWN)), device_id_type=MESH)

    def z_near(i):
        return (zq * 4 + lax.rem(zi + i, 4), p)

    def z_far(i):
        return (lax.rem(g + 4 * i, NZ), p)

    for i in (1, 2, 3):
        pl.semaphore_signal(barrier, inc=1, device_id=z_near(i), device_id_type=MESH)
    for i in (1, 2):
        pl.semaphore_signal(barrier, inc=1, device_id=z_far(i), device_id_type=MESH)

    for load in loads[:1]:
        load.wait()

    @pl.loop(0, 8)
    def _(b):
        some = ups_v[pl.ds(b * 32, 32)].astype(F32)
        for t in range(4):
            wide[t, pl.ds(pl.multiple_of(b * 128, 128), 128), :] = some[:, :, t * 128 : t * 128 + 128].reshape(128, 128)

    for c in range(4):
        for t in range(4):
            uc_v[c, :, t * 128 : t * 128 + 128] = wide[t, pl.ds(c, GB, stride=4), :].astype(BF16)

    loads[1].wait()

    def term(lo, hi, c):
        return lax.dot_general(
            pooled_v[:, lo:hi], uc_v[c], (((0,), (0,)), ((), ())), preferred_element_type=F32
        )

    def keep(half, row, value):
        for part in range(2):
            acc[half, part, row : row + value.shape[0], :] = value[:, part * 256 : part * 256 + 256]

    keep(0, 0, term(384, 960, 3)[64:576])
    keep(1, 0, term(0, 128, 0))
    keep(1, 128, term(0, 256, 1)[64:192])
    keep(1, 256, term(128, 512, 2)[64:320])

    pl.semaphore_wait(barrier, N_OWN - 1 + 5)

    def span(kind, i):
        if kind == "x":
            t = lax.rem(xi + i, NX)
            return t, pl.ds(pl.multiple_of(t * 128, 128), 128)
        t = lax.rem(yi + i, NY)
        return t, pl.ds(pl.multiple_of(t * 64, 64), 64)

    def part_of(kind):
        return 0 if kind == "x" else 1

    sib_dev = at(yi, xi, other)
    steps = BOTH + (("x", 0), ("y", 0))
    sib_copies = {}
    for n, (kind, i) in enumerate(steps):
        t, rows = span(kind, i)
        part = part_of(kind)
        copy = remote(acc.at[other, part, rows], sib.at[part, rows], sib_s.at[n], sib_r.at[n], sib_dev)
        copy.start()
        sib_copies[kind, i] = copy

    def chip_sum(kind, i):
        t, rows = span(kind, i)
        part = part_of(kind)
        return acc[core, part, rows, :] + sib[part, rows, :]

    first = {}
    for kind, i in BOTH:
        sib_copies[kind, i].wait_recv()
        t, rows = span(kind, i)
        if kind == "x":
            pack(tiles_of(chip_sum(kind, i)), x1s.at[i - 1])
            copy = remote(x1s.at[i - 1], x1r.at[i - 1], x1_s.at[i - 1], x1_r.at[i - 1], at(yi, t, core))
        else:
            pack(tiles_of(chip_sum(kind, i)), y1s.at[i - 1])
            copy = remote(y1s.at[i - 1], y1r.at[i - 1], y1_s.at[i - 1], y1_r.at[i - 1], at(t, xi, core))
        copy.start()
        first[kind, i] = copy

    loads[2].wait()
    for c, ((offset, width), (block, number)) in enumerate(zip(CLASSES, BLOCKS)):
        bag = lax.dot_general(
            uc_v[c], proj_v[offset : offset + number * 128], (((1,), (1,)), ((), ())),
            preferred_element_type=F32,
        )
        for k in range(number):
            for s in range(4):
                stage[pl.ds(s * 8 + block + k, N_OWN, stride=32), :] = bag[
                    s * 64 : s * 64 + 64, k * 128 : k * 128 + 128
                ]
    abuf[...] = stage[...].reshape(N_OWN, 32, 128).astype(BF16)

    loads[3].wait()
    loads[4].wait()
    spread = lax.broadcasted_iota(jnp.int32, (GB, GB), 0)
    order = (spread & 63) * 4 + (spread >> 6)
    picked = jnp.where(order == lax.broadcasted_iota(jnp.int32, (GB, GB), 1), 1.0, 0.0).astype(BF16)
    for member in range(4):
        valid = lax.broadcasted_iota(jnp.int32, (BAG, GB), 0) < sizes_v[member : member + 1, :]
        wanted = jnp.where(valid, looks_v[member], -1)
        parts = []
        for r in range(0, GB, 64):
            ids = lax.broadcasted_iota(jnp.int32, (64, GB), 0) + r
            count = jnp.zeros((64, GB), F32)
            for l in range(BAG):
                count += jnp.where(wanted[l : l + 1, :] == ids, 1.0, 0.0)
            parts.append(count.astype(BF16))
        counts = jnp.concatenate(parts, axis=0)
        tal[member] = lax.dot_general(
            picked, counts, (((1,), (1,)), ((), ())), preferred_element_type=F32
        ).astype(BF16)

    second = {}
    sib_copies["x", 0].wait_recv()
    total = tiles_of(chip_sum("x", 0))
    for i in X_ORDER:
        first["x", i].wait_recv()
        total = [a + b for a, b in zip(total, unpack(x1r.at[i - 1], 16))]
    for k, tile in enumerate(total):
        y2s[k // 2, :, (k % 2) * 128 : (k % 2) * 128 + 128] = tile
    for i in Y_ORDER:
        t, rows = span("y", i)
        copy = remote(y2s.at[t], y2r.at[i - 1], y2_s.at[i - 1], y2_r.at[i - 1], at(t, xi, core))
        copy.start()
        second["y", i] = copy
    sib_copies["y", 0].wait_recv()
    total = tiles_of(chip_sum("y", 0))
    for i in Y_ORDER:
        first["y", i].wait_recv()
        total = [a + b for a, b in zip(total, unpack(y1r.at[i - 1], 8))]
    for k, tile in enumerate(total):
        x2s[k // 2, :, (k % 2) * 128 : (k % 2) * 128 + 128] = tile
    for i in X_ORDER:
        t, rows = span("x", i)
        copy = remote(x2s.at[t], x2r.at[i - 1], x2_s.at[i - 1], x2_r.at[i - 1], at(yi, t, core))
        copy.start()
        second["x", i] = copy

    def to_owner(i):
        t = lax.rem(p + i, N_OWN)
        return remote(abuf.at[t], arecv.at[p], a_s, a_r, (g, t))

    @pl.loop(1, N_OWN)
    def _(i):
        to_owner(i).start()

    arecv[p] = abuf[p]

    part = y2s[yi]
    for i in Y_ORDER:
        second["y", i].wait_recv()
        part += y2r[i - 1]
    z1[zi, :, 0:256] = part
    part = x2s[xi]
    for i in X_ORDER:
        second["x", i].wait_recv()
        part += x2r[i - 1]
    z1[zi, :, 256:512] = part

    z1_copies = []
    for i in (1, 2, 3):
        copy = remote(z1.at[zi], z1.at[zi], z1_s.at[i - 1], z1_r.at[i - 1], z_near(i))
        copy.start()
        z1_copies.append(copy)
    for copy in z1_copies:
        copy.wait_recv()
    z2[zq] = (z1[0] + z1[1]) + (z1[2] + z1[3])
    z2_copies = []
    for i in (1, 2):
        copy = remote(z2.at[zq], z2.at[zq], z2_s.at[i - 1], z2_r.at[i - 1], z_far(i))
        copy.start()
        z2_copies.append(copy)
    for copy in z2_copies:
        copy.wait_recv()
    whole = ((z2[0] + z2[1]) + z2[2]) * scale

    ga[yi] = whole[:, 0:256]
    gb[xi] = whole[:, 256:512]
    back = {}
    for i in X_ORDER:
        t, rows = span("x", i)
        back["x", i] = remote(gb.at[xi], gb.at[xi], gb_s.at[i - 1], gb_r.at[i - 1], at(yi, t, core))
        back["x", i].start()
    for i in Y_ORDER:
        t, rows = span("y", i)
        back["y", i] = remote(ga.at[yi], ga.at[yi], ga_s.at[i - 1], ga_r.at[i - 1], at(t, xi, core))
        back["y", i].start()

    pltpu.make_async_copy(arecv.at[pl.ds(0, N_OWN - 1)], arecv.at[pl.ds(0, N_OWN - 1)], a_r).wait()
    loads[5].wait()
    loads[6].wait()
    stage[...] = arecv[...].astype(F32).reshape(N_OWN * 32, 128)
    for member, ((offset, width), (block, number)) in enumerate(zip(CLASSES, BLOCKS)):
        columns = []
        for k in range(number):
            columns.append(
                jnp.concatenate(
                    [stage[pl.ds(s * 8 + block + k, N_OWN, stride=32), :] for s in range(4)], axis=0
                ).astype(BF16)
            )
        bags = columns[0] if number == 1 else jnp.concatenate(columns, axis=1)
        grad = lax.dot_general(
            bags, tal[member], (((0,), (0,)), ((), ())), preferred_element_type=F32
        )[:width]
        new = state_v[member : member + 1, :] + jnp.sum(grad * grad, axis=0, keepdims=True) * (1.0 / width)
        state_out[member : member + 1, :] = new
        rows_out[offset : offset + width, :] = emb_v[offset : offset + width, :] - grad * (LEARN / jnp.sqrt(new))
    last = {}
    hand = {}

    def slot(kind, half, t):
        return gx.at[half, t] if kind == "x" else gy.at[half, t]

    def to_other(kind, i, t):
        sems = (hx_s.at[i], hx_r.at[i]) if kind == "x" else (hy_s.at[i], hy_r.at[i])
        hand[kind, i] = remote(slot(kind, core, t), slot(kind, core, t), *sems, sib_dev)
        hand[kind, i].start()

    def put(kind, half, t):
        top = (1 - half) * 32
        number, left = (16, 0) if kind == "x" else (8, 256)
        for k, tile in enumerate(unpack(slot(kind, half, t), number)):
            column = left + (k % 2) * 128
            pg_out[top + t * (number // 2) + k // 2, :, column : column + 128] = tile

    def spread_out(kind, i):
        t, rows = span(kind, i)
        if kind == "x":
            sems, dev = (gx_s.at[i - 1], gx_r.at[i - 1]), at(yi, t, core)
            mine = slot("x", core, xi)
        else:
            sems, dev = (gy_s.at[i - 1], gy_r.at[i - 1]), at(t, xi, core)
            mine = slot("y", core, yi)
        last[kind, i] = remote(mine, mine, *sems, dev)
        last[kind, i].start()

    for i in X_ORDER:
        back["x", i].wait_recv()
    pack([gb[k // 2, :, (k % 2) * 128 : (k % 2) * 128 + 128] for k in range(8)], slot("y", core, yi))
    for i in Y_ORDER:
        spread_out("y", i)
    to_other("y", 0, yi)
    for i in Y_ORDER:
        back["y", i].wait_recv()
    pack([ga[k // 2, :, (k % 2) * 128 : (k % 2) * 128 + 128] for k in range(16)], slot("x", core, xi))
    for i in X_ORDER:
        spread_out("x", i)
    to_other("x", 0, xi)
    put("y", core, yi)
    put("x", core, xi)
    for kind, i in BOTH:
        last[kind, i].wait_recv()
        t = lax.rem(xi - i + NX, NX) if kind == "x" else lax.rem(yi - i + NY, NY)
        to_other(kind, i, t)
        put(kind, core, t)
    for kind, i in (("y", 0), ("x", 0)) + BOTH:
        hand[kind, i].wait_recv()
        t = lax.rem(xi - i + NX, NX) if kind == "x" else lax.rem(yi - i + NY, NY)
        put(kind, other, t)

    for group in (sib_copies, first, second, back, last, hand):
        for copy in group.values():
            copy.wait_send()
    for copy in z1_copies + z2_copies:
        copy.wait_send()

    @pl.loop(1, N_OWN)
    def _(i):
        to_owner(i).wait_send()


def on_device(upstream, pooled, projection, embedding, row_state, lookups, bag_sizes):
    total_bags = upstream.shape[0] * lax.axis_size("grp") * lax.axis_size("own") * upstream.shape[1]
    scale = 1.0 / math.sqrt(total_bags)
    operands = (
        upstream.reshape(GB, 4, 512), pooled.reshape(GB, 960), projection, embedding.T, row_state,
        jnp.transpose(lookups[0], (0, 2, 1)), bag_sizes[0],
    )
    dma = pltpu.SemaphoreType.DMA
    any_space = pl.BlockSpec(memory_space=pl.ANY)
    scratch = [pltpu.VMEM(a.shape, a.dtype) for a in operands] + [
        pltpu.VMEM((2, 2, 512, 256), F32),
        pltpu.VMEM((2, 512, 256), F32),
        pltpu.VMEM((3, 17, 16, 128), I16),
        pltpu.VMEM((3, 17, 16, 128), I16),
        pltpu.VMEM((7, 9, 16, 128), I16),
        pltpu.VMEM((7, 9, 16, 128), I16),
        pltpu.VMEM((8, 16, 256), F32),
        pltpu.VMEM((7, 16, 256), F32),
        pltpu.VMEM((4, 16, 256), F32),
        pltpu.VMEM((3, 16, 256), F32),
        pltpu.VMEM((4, 16, 512), F32),
        pltpu.VMEM((3, 16, 512), F32),
        pltpu.VMEM((8, 16, 256), F32),
        pltpu.VMEM((4, 16, 256), F32),
        pltpu.VMEM((2, 4, 17, 16, 128), I16),
        pltpu.VMEM((2, 8, 9, 16, 128), I16),
        pltpu.VMEM((4, 4 * GB, 128), F32),
        pltpu.VMEM((4, GB, 512), BF16),
        pltpu.VMEM((N_OWN * 32, 128), F32),
        pltpu.VMEM((N_OWN, 32, 128), BF16),
        pltpu.VMEM((N_OWN, 32, 128), BF16),
        pltpu.VMEM((4, GB, GB), BF16),
    ] + [
        dma(() if n == 0 else (n,))
        for n in (7, 12, 12, 3, 3, 7, 7, 7, 7, 3, 3, 3, 3, 2, 2, 0, 0, 7, 7, 3, 3, 3, 3, 7, 7, 4, 4, 8, 8)
    ]
    rows_t, new_state, pg = pl.pallas_call(
        functools.partial(kernel, scale),
        out_shape=(
            pltpu.VMEM((960, GB), F32),
            pltpu.VMEM((4, GB), F32),
            pltpu.VMEM((64, 16, 512), F32),
        ),
        in_specs=[pl.BlockSpec(memory_space=pltpu.HBM)] * len(operands),
        out_specs=(pl.BlockSpec(memory_space=pltpu.VMEM),) * 3,
        scratch_shapes=scratch,
        compiler_params=pltpu.CompilerParams(
            collective_id=0, has_side_effects=True, vmem_limit_bytes=54 * 2**20
        ),
        name="fused",
    )(*operands)
    pg = jnp.concatenate([pg[0:4], pg[8:64]], axis=0).reshape(960, 512)
    return rows_t.T, new_state, pg


def solution(mesh):
    return jax.shard_map(
        on_device,
        mesh=mesh,
        in_specs=(
            P(("grp", "own"), None, None, None),
            P(("grp", "own"), None, None),
            P(),
            P(("grp", "own"), None),
            P(None, ("grp", "own")),
            P(("grp", "own"), None, None, None),
            P(("grp", "own"), None, None),
        ),
        out_specs=(P(("grp", "own"), None), P(None, ("grp", "own")), P()),
        check_vma=False,
    )
```

time: 169 us -> 64.4 us (0.38)
  Pallas kernels: 166 us -> 60.3 us
    pallas_call x1 -> x0, Pallas kernels: 90.6 us -> none  [on_device(): pl.pallas_call(flush, out_shape=tuple((jax.ShapeDtypeStruct(a.shape, a.dt...]
    pallas_call x1, Pallas kernels: 75.3 us -> 60.3 us  [on_device(): pl.pallas_call(functools.partial(kernel, scale), out_shape=(pltpu.VMEM((9...]
where the time goes in v3:
time: 64.4 us; the launch traced here: 64.2 us
  Pallas kernels  60.3 us (94%)
  local copies, waits for them, and re-layouts  1.77 us (3%)
  other arithmetic  1.51 us (2%)
  between operations  0.65 us (1%)
    pallas_call x1, Pallas kernels, on_device(): pl.pallas_call(functools.partial(kernel, scale), out_shape=(pltpu.VMEM((9...  60.3 us
    unnamed x2, local copies, waits for them, and re-layouts  1.54 us
    concatenate x1, other arithmetic, on_device(): pg = jnp.concatenate([pg[0:4], pg[8:64]], axis=0).reshape(960, 512)  1.51 us

profile of v3, /device:TPU:1, one launch (start us, length us, event | category | flops | bytes accessed | tf_op | source)
XLA Modules:
  0.0 64.2 jit_solution(2578675316518731202)
XLA Ops:
  0.6 60.3 %fused.1 = (f32[960,256]{1,0:T(8,128)S(1)}, f32[4,256]{1,0:T(4,128)S(1)}, f32[64,16,512]{2,1,0:T(8,128)S(1)}) custom-call(bf16[256,4,512]{2,1,0:T(4,128)(2,1)} %bitcast.11, bf16[256,960]{1,0:T(8,128)(2,1)} %bitcast.13, bf16[960,512]{1,0:T(8,128)(2,1)} %proj.1, f32[960,256]{1,0:T(8,128)} %bitcast.12, f32[4,256]{1,0:T(4,128)} %state.1, ...), custom_call_target="tpu_custom_call" | custom-call | tf_op jit(solution)/shard_map/fused/pallas_call | solution.py:402
  60.9 0.9 %copy.12 = f32[256,960]{0,1:T(8,128)} copy(f32[256,960]{0,1:T(8,128)S(1)} %bitcast.9) | data formatting | bytes 1966080
  61.9 0.6 copy.13
  62.5 0.2 slice.7
  62.7 1.5 %pad_maximum_fusion = f32[60,16,512]{2,1,0:T(8,128)} fusion(f32[56,16,512]{2,1,0:T(8,128)S(1)} %slice.7, f32[4,16,512]{2,1,0:T(8,128)S(1)} %slice.6), kind=kLoop, calls=%fused_computation | loop fusion | flops 491520 | bytes 3932160 | tf_op jit(solution)/shard_map/concatenate | solution.py:417
  (1 shorter events, 0.0 us)

commit v4 on v3

--- a/solution.py
+++ b/solution.py
@@ -81,26 +81,27 @@
     ins = (
         (ups, ups_v), (pooled, pooled_v), (proj, proj_v), (looks, looks_v), (sizes, sizes_v), (emb, emb_v), (state, state_v),
     )
+    barrier = pltpu.get_barrier_semaphore()
+
+    def z_near(i):
+        return (zq * 4 + lax.rem(zi + i, 4), p)
+
+    def z_far(i):
+        return (lax.rem(g + 4 * i, NZ), p)
+
+    partners = (
+        [at(lax.rem(yi + i, NY), xi, core) for i in Y_ORDER]
+        + [at(yi, lax.rem(xi + i, NX), core) for i in X_ORDER]
+        + [at(yi, xi, other)]
+        + [z_far(i) for i in (1, 2)]
+        + [z_near(i) for i in (2, 1, 3)]
+    )
+    for dev in partners:
+        pl.semaphore_signal(barrier, inc=1, device_id=dev, device_id_type=MESH)
+
     loads = [pltpu.make_async_copy(a, b, in_sem.at[i]) for i, (a, b) in enumerate(ins)]
     for load in loads:
         load.start()
-
-    barrier = pltpu.get_barrier_semaphore()
-
-    @pl.loop(1, N_OWN)
-    def _(i):
-        pl.semaphore_signal(barrier, inc=1, device_id=(g, lax.rem(p + i, N_OWN)), device_id_type=MESH)
-
-    def z_near(i):
-        return (zq * 4 + lax.rem(zi + i, 4), p)
-
-    def z_far(i):
-        return (lax.rem(g + 4 * i, NZ), p)
-
-    for i in (1, 2, 3):
-        pl.semaphore_signal(barrier, inc=1, device_id=z_near(i), device_id_type=MESH)
-    for i in (1, 2):
-        pl.semaphore_signal(barrier, inc=1, device_id=z_far(i), device_id_type=MESH)
 
     for load in loads[:1]:
         load.wait()
@@ -131,7 +132,7 @@
     keep(1, 128, term(0, 256, 1)[64:192])
     keep(1, 256, term(128, 512, 2)[64:320])
 
-    pl.semaphore_wait(barrier, N_OWN - 1 + 5)
+    pl.semaphore_wait(barrier, len(partners))
 
     def span(kind, i):
         if kind == "x":
@@ -230,56 +231,116 @@
         copy.start()
         second["x", i] = copy
 
+    def near(n, mine):
+        copies = []
+        z1[n, zi] = mine
+        for i in (3, 2, 1):
+            slot = z1.at[n, zi]
+            copies.append(remote(slot, slot, z1_s.at[n, i - 1], z1_r.at[n, i - 1], z_near(i)))
+            copies[-1].start()
+        return copies
+
+    def far(n):
+        copies = []
+        z2[n, zq] = (z1[n, 0] + z1[n, 1]) + (z1[n, 2] + z1[n, 3])
+        for i in (1, 2):
+            slot = z2.at[n, zq]
+            copies.append(remote(slot, slot, z2_s.at[n, i - 1], z2_r.at[n, i - 1], z_far(i)))
+            copies[-1].start()
+        return copies
+
     def to_owner(i):
         t = lax.rem(p + i, N_OWN)
         return remote(abuf.at[t], arecv.at[p], a_s, a_r, (g, t))
 
-    @pl.loop(1, N_OWN)
-    def _(i):
-        to_owner(i).start()
-
-    arecv[p] = abuf[p]
-
-    part = y2s[yi]
+    def send_bags():
+        @pl.loop(1, N_OWN)
+        def _(i):
+            to_owner(i).start()
+
+        arecv[p] = abuf[p]
+
+    z_copies = []
+    waiting = []
+    for n, (order, kind, own, got) in enumerate(((Y_ORDER, "y", y2s, y2r), (X_ORDER, "x", x2s, x2r))):
+        part = own[yi if kind == "y" else xi]
+        for i in order:
+            second[kind, i].wait_recv()
+            part += got[i - 1]
+        waiting.append(near(n, part))
+        z_copies += waiting[-1]
+        if n == 0:
+            send_bags()
+
+    for n in range(2):
+        for copy in waiting[n]:
+            copy.wait_recv()
+        waiting[n] = far(n)
+        z_copies += waiting[n]
+
+    back = {}
+    for n, (order, kind, gathered) in enumerate(((Y_ORDER, "y", ga), (X_ORDER, "x", gb))):
+        for copy in waiting[n]:
+            copy.wait_recv()
+        here = yi if kind == "y" else xi
+        gathered[here] = ((z2[n, 0] + z2[n, 1]) + z2[n, 2]) * scale
+        for i in order:
+            t, rows = span(kind, i)
+            if kind == "y":
+                sems, dev = (ga_s.at[i - 1], ga_r.at[i - 1]), at(t, xi, core)
+            else:
+                sems, dev = (gb_s.at[i - 1], gb_r.at[i - 1]), at(yi, t, core)
+            back[kind, i] = remote(gathered.at[here], gathered.at[here], *sems, dev)
+            back[kind, i].start()
+
+    last = {}
+    hand = {}
+
+    def slot(kind, half, t):
+        return gx.at[half, t] if kind == "x" else gy.at[half, t]
+
+    def to_other(kind, i, t):
+        sems = (hx_s.at[i], hx_r.at[i]) if kind == "x" else (hy_s.at[i], hy_r.at[i])
+        hand[kind, i] = remote(slot(kind, core, t), slot(kind, core, t), *sems, sib_dev)
+        hand[kind, i].start()
+
+    def put(kind, half, t):
+        number, left, groups = (16, 0, 8) if kind == "x" else (8, 256, 4)
+        later = (t + 7) // 8 if kind == "y" else (t + 3) // 4
+        for k, tile in enumerate(unpack(slot(kind, half, t), number)):
+            column = left + (k % 2) * 128
+            r = k // 2
+            plain = t * groups + r
+            if kind == "x":
+                moved = plain - 4 * later + (0 if r < 4 else 56 * (1 - later))
+            else:
+                moved = plain - 4 * later + 60 * (later - (t + 6) // 8)
+            row = half * moved + (1 - half) * (plain + 28)
+            pg_out[row, :, column : column + 128] = tile
+
+    def spread_out(kind, i):
+        t, rows = span(kind, i)
+        if kind == "x":
+            sems, dev = (gx_s.at[i - 1], gx_r.at[i - 1]), at(yi, t, core)
+            mine = slot("x", core, xi)
+        else:
+            sems, dev = (gy_s.at[i - 1], gy_r.at[i - 1]), at(t, xi, core)
+            mine = slot("y", core, yi)
+        last[kind, i] = remote(mine, mine, *sems, dev)
+        last[kind, i].start()
+
+    for i in X_ORDER:
+        back["x", i].wait_recv()
+    pack([gb[k // 2, :, (k % 2) * 128 : (k % 2) * 128 + 128] for k in range(8)], slot("y", core, yi))
     for i in Y_ORDER:
-        second["y", i].wait_recv()
-        part += y2r[i - 1]
-    z1[zi, :, 0:256] = part
-    part = x2s[xi]
+        spread_out("y", i)
+    to_other("y", 0, yi)
+    for i in Y_ORDER:
+        back["y", i].wait_recv()
+    pack([ga[k // 2, :, (k % 2) * 128 : (k % 2) * 128 + 128] for k in range(16)], slot("x", core, xi))
     for i in X_ORDER:
-        second["x", i].wait_recv()
-        part += x2r[i - 1]
-    z1[zi, :, 256:512] = part
-
-    z1_copies = []
-    for i in (1, 2, 3):
-        copy = remote(z1.at[zi], z1.at[zi], z1_s.at[i - 1], z1_r.at[i - 1], z_near(i))
-        copy.start()
-        z1_copies.append(copy)
-    for copy in z1_copies:
-        copy.wait_recv()
-    z2[zq] = (z1[0] + z1[1]) + (z1[2] + z1[3])
-    z2_copies = []
-    for i in (1, 2):
-        copy = remote(z2.at[zq], z2.at[zq], z2_s.at[i - 1], z2_r.at[i - 1], z_far(i))
-        copy.start()
-        z2_copies.append(copy)
-    for copy in z2_copies:
-        copy.wait_recv()
-    whole = ((z2[0] + z2[1]) + z2[2]) * scale
-
-    ga[yi] = whole[:, 0:256]
-    gb[xi] = whole[:, 256:512]
-    back = {}
-    for i in X_ORDER:
-        t, rows = span("x", i)
-        back["x", i] = remote(gb.at[xi], gb.at[xi], gb_s.at[i - 1], gb_r.at[i - 1], at(yi, t, core))
-        back["x", i].start()
-    for i in Y_ORDER:
-        t, rows = span("y", i)
-        back["y", i] = remote(ga.at[yi], ga.at[yi], ga_s.at[i - 1], ga_r.at[i - 1], at(t, xi, core))
-        back["y", i].start()
-
+        spread_out("x", i)
+    to_other("x", 0, xi)
     pltpu.make_async_copy(arecv.at[pl.ds(0, N_OWN - 1)], arecv.at[pl.ds(0, N_OWN - 1)], a_r).wait()
     loads[5].wait()
     loads[6].wait()
@@ -299,47 +360,6 @@
         new = state_v[member : member + 1, :] + jnp.sum(grad * grad, axis=0, keepdims=True) * (1.0 / width)
         state_out[member : member + 1, :] = new
         rows_out[offset : offset + width, :] = emb_v[offset : offset + width, :] - grad * (LEARN / jnp.sqrt(new))
-    last = {}
-    hand = {}
-
-    def slot(kind, half, t):
-        return gx.at[half, t] if kind == "x" else gy.at[half, t]
-
-    def to_other(kind, i, t):
-        sems = (hx_s.at[i], hx_r.at[i]) if kind == "x" else (hy_s.at[i], hy_r.at[i])
-        hand[kind, i] = remote(slot(kind, core, t), slot(kind, core, t), *sems, sib_dev)
-        hand[kind, i].start()
-
-    def put(kind, half, t):
-        top = (1 - half) * 32
-        number, left = (16, 0) if kind == "x" else (8, 256)
-        for k, tile in enumerate(unpack(slot(kind, half, t), number)):
-            column = left + (k % 2) * 128
-            pg_out[top + t * (number // 2) + k // 2, :, column : column + 128] = tile
-
-    def spread_out(kind, i):
-        t, rows = span(kind, i)
-        if kind == "x":
-            sems, dev = (gx_s.at[i - 1], gx_r.at[i - 1]), at(yi, t, core)
-            mine = slot("x", core, xi)
-        else:
-            sems, dev = (gy_s.at[i - 1], gy_r.at[i - 1]), at(t, xi, core)
-            mine = slot("y", core, yi)
-        last[kind, i] = remote(mine, mine, *sems, dev)
-        last[kind, i].start()
-
-    for i in X_ORDER:
-        back["x", i].wait_recv()
-    pack([gb[k // 2, :, (k % 2) * 128 : (k % 2) * 128 + 128] for k in range(8)], slot("y", core, yi))
-    for i in Y_ORDER:
-        spread_out("y", i)
-    to_other("y", 0, yi)
-    for i in Y_ORDER:
-        back["y", i].wait_recv()
-    pack([ga[k // 2, :, (k % 2) * 128 : (k % 2) * 128 + 128] for k in range(16)], slot("x", core, xi))
-    for i in X_ORDER:
-        spread_out("x", i)
-    to_other("x", 0, xi)
     put("y", core, yi)
     put("x", core, xi)
     for kind, i in BOTH:
@@ -355,7 +375,7 @@
     for group in (sib_copies, first, second, back, last, hand):
         for copy in group.values():
             copy.wait_send()
-    for copy in z1_copies + z2_copies:
+    for copy in z_copies:
         copy.wait_send()
 
     @pl.loop(1, N_OWN)
@@ -383,8 +403,8 @@
         pltpu.VMEM((7, 16, 256), F32),
         pltpu.VMEM((4, 16, 256), F32),
         pltpu.VMEM((3, 16, 256), F32),
-        pltpu.VMEM((4, 16, 512), F32),
-        pltpu.VMEM((3, 16, 512), F32),
+        pltpu.VMEM((2, 4, 16, 256), F32),
+        pltpu.VMEM((2, 3, 16, 256), F32),
         pltpu.VMEM((8, 16, 256), F32),
         pltpu.VMEM((4, 16, 256), F32),
         pltpu.VMEM((2, 4, 17, 16, 128), I16),
@@ -396,8 +416,8 @@
         pltpu.VMEM((N_OWN, 32, 128), BF16),
         pltpu.VMEM((4, GB, GB), BF16),
     ] + [
-        dma(() if n == 0 else (n,))
-        for n in (7, 12, 12, 3, 3, 7, 7, 7, 7, 3, 3, 3, 3, 2, 2, 0, 0, 7, 7, 3, 3, 3, 3, 7, 7, 4, 4, 8, 8)
+        dma(n if isinstance(n, tuple) else () if n == 0 else (n,))
+        for n in (7, 12, 12, 3, 3, 7, 7, 7, 7, 3, 3, (2, 3), (2, 3), (2, 2), (2, 2), 0, 0, 7, 7, 3, 3, 3, 3, 7, 7, 4, 4, 8, 8)
     ]
     rows_t, new_state, pg = pl.pallas_call(
         functools.partial(kernel, scale),
@@ -414,8 +434,7 @@
         ),
         name="fused",
     )(*operands)
-    pg = jnp.concatenate([pg[0:4], pg[8:64]], axis=0).reshape(960, 512)
-    return rows_t.T, new_state, pg
+    return rows_t.T, new_state, pg[0:60].reshape(960, 512)
 
 
 def solution(mesh):

time: 64.4 us -> 61.8 us (0.960)
  Pallas kernels: 60.3 us -> 57.9 us
  other arithmetic: 1.51 us -> 0 us
  local copies, waits for them, and re-layouts: 1.77 us -> 3.09 us
    pallas_call x1, Pallas kernels: 60.3 us -> 57.9 us  [on_device(): pl.pallas_call(functools.partial(kernel, scale), out_shape=(pltpu.VMEM((9...]
    concatenate x1 -> x0, other arithmetic: 1.51 us -> none  [on_device(): pg = jnp.concatenate([pg[0:4], pg[8:64]], axis=0).reshape(960, 512)]
    slice x2 -> x1, local copies, waits for them, and re-layouts: 0.23 us -> 1.55 us  [on_device(): return (rows_t.T, new_state, pg[0:60].reshape(960, 512))]
where the time goes in v4:
time: 61.8 us; the launch traced here: 61.6 us
  Pallas kernels  57.9 us (94%)
  local copies, waits for them, and re-layouts  3.09 us (5%)
  between operations  0.64 us (1%)
    pallas_call x1, Pallas kernels, on_device(): pl.pallas_call(functools.partial(kernel, scale), out_shape=(pltpu.VMEM((9...  57.9 us
    slice x1, local copies, waits for them, and re-layouts, on_device(): return (rows_t.T, new_state, pg[0:60].reshape(960, 512))  1.55 us
    unnamed x2, local copies, waits for them, and re-layouts  1.54 us

profile of v4, /device:TPU:1, one launch (start us, length us, event | category | flops | bytes accessed | tf_op | source)
XLA Modules:
  0.0 61.6 jit_solution(13322291804430937325)
XLA Ops:
  0.6 57.9 %fused.1 = (f32[960,256]{1,0:T(8,128)S(1)}, f32[4,256]{1,0:T(4,128)S(1)}, f32[64,16,512]{2,1,0:T(8,128)S(1)}) custom-call(bf16[256,4,512]{2,1,0:T(4,128)(2,1)} %bitcast.11, bf16[256,960]{1,0:T(8,128)(2,1)} %bitcast.13, bf16[960,512]{1,0:T(8,128)(2,1)} %proj.1, f32[960,256]{1,0:T(8,128)} %bitcast.12, f32[4,256]{1,0:T(4,128)} %state.1, ...), custom_call_target="tpu_custom_call" | custom-call | tf_op jit(solution)/shard_map/fused/pallas_call | solution.py:422
  58.5 0.9 %copy.12 = f32[256,960]{0,1:T(8,128)} copy(f32[256,960]{0,1:T(8,128)S(1)} %bitcast.9) | data formatting | bytes 1966080
  59.5 0.6 copy.13
  60.1 1.6 %slice.3 = f32[60,16,512]{2,1,0:T(8,128)} slice(f32[64,16,512]{2,1,0:T(8,128)S(1)} %get-tuple-element.8), slice={[0:60], [0:16], [0:512]} | slice | bytes 3932160 | tf_op jit(solution)/shard_map/slice | solution.py:437

commit v5 on v4

--- a/solution.py
+++ b/solution.py
@@ -23,7 +23,7 @@
 I16 = jnp.int16
 X_ORDER = (2, 1, 3)
 Y_ORDER = (4, 3, 5, 2, 6, 1, 7)
-BOTH = (("y", 4), ("y", 3), ("x", 2), ("y", 5), ("y", 2), ("x", 1), ("y", 6), ("y", 1), ("x", 3), ("y", 7))
+BOTH = (("y", 4), ("y", 3), ("y", 5), ("y", 2), ("x", 2), ("y", 6), ("y", 1), ("x", 1), ("y", 7), ("x", 3))
 
 
 def pack(tiles, q):
@@ -211,8 +211,8 @@
     for i in X_ORDER:
         first["x", i].wait_recv()
         total = [a + b for a, b in zip(total, unpack(x1r.at[i - 1], 16))]
-    for k, tile in enumerate(total):
-        y2s[k // 2, :, (k % 2) * 128 : (k % 2) * 128 + 128] = tile
+    for k in range(8):
+        pack(total[2 * k : 2 * k + 2], y2s.at[k])
     for i in Y_ORDER:
         t, rows = span("y", i)
         copy = remote(y2s.at[t], y2r.at[i - 1], y2_s.at[i - 1], y2_r.at[i - 1], at(t, xi, core))
@@ -223,17 +223,23 @@
     for i in Y_ORDER:
         first["y", i].wait_recv()
         total = [a + b for a, b in zip(total, unpack(y1r.at[i - 1], 8))]
-    for k, tile in enumerate(total):
-        x2s[k // 2, :, (k % 2) * 128 : (k % 2) * 128 + 128] = tile
+    for k in range(4):
+        pack(total[2 * k : 2 * k + 2], x2s.at[k])
     for i in X_ORDER:
         t, rows = span("x", i)
         copy = remote(x2s.at[t], x2r.at[i - 1], x2_s.at[i - 1], x2_r.at[i - 1], at(yi, t, core))
         copy.start()
         second["x", i] = copy
 
+    def summed(terms):
+        total = unpack(terms[0], 2)
+        for term in terms[1:]:
+            total = [a + b for a, b in zip(total, unpack(term, 2))]
+        return total
+
     def near(n, mine):
         copies = []
-        z1[n, zi] = mine
+        pack(mine, z1.at[n, zi])
         for i in (3, 2, 1):
             slot = z1.at[n, zi]
             copies.append(remote(slot, slot, z1_s.at[n, i - 1], z1_r.at[n, i - 1], z_near(i)))
@@ -242,7 +248,7 @@
 
     def far(n):
         copies = []
-        z2[n, zq] = (z1[n, 0] + z1[n, 1]) + (z1[n, 2] + z1[n, 3])
+        pack(summed([z1.at[n, i] for i in range(4)]), z2.at[n, zq])
         for i in (1, 2):
             slot = z2.at[n, zq]
             copies.append(remote(slot, slot, z2_s.at[n, i - 1], z2_r.at[n, i - 1], z_far(i)))
@@ -263,10 +269,9 @@
     z_copies = []
     waiting = []
     for n, (order, kind, own, got) in enumerate(((Y_ORDER, "y", y2s, y2r), (X_ORDER, "x", x2s, x2r))):
-        part = own[yi if kind == "y" else xi]
         for i in order:
             second[kind, i].wait_recv()
-            part += got[i - 1]
+        part = summed([own.at[yi if kind == "y" else xi]] + [got.at[i - 1] for i in order])
         waiting.append(near(n, part))
         z_copies += waiting[-1]
         if n == 0:
@@ -283,7 +288,7 @@
         for copy in waiting[n]:
             copy.wait_recv()
         here = yi if kind == "y" else xi
-        gathered[here] = ((z2[n, 0] + z2[n, 1]) + z2[n, 2]) * scale
+        pack([tile * scale for tile in summed([z2.at[n, i] for i in range(3)])], gathered.at[here])
         for i in order:
             t, rows = span(kind, i)
             if kind == "y":
@@ -306,17 +311,27 @@
 
     def put(kind, half, t):
         number, left, groups = (16, 0, 8) if kind == "x" else (8, 256, 4)
-        later = (t + 7) // 8 if kind == "y" else (t + 3) // 4
-        for k, tile in enumerate(unpack(slot(kind, half, t), number)):
-            column = left + (k % 2) * 128
-            r = k // 2
-            plain = t * groups + r
-            if kind == "x":
-                moved = plain - 4 * later + (0 if r < 4 else 56 * (1 - later))
-            else:
-                moved = plain - 4 * later + 60 * (later - (t + 6) // 8)
-            row = half * moved + (1 - half) * (plain + 28)
-            pg_out[row, :, column : column + 128] = tile
+        tiles = unpack(slot(kind, half, t), number)
+
+        def store(low, high, row):
+            for k in range(2 * low, 2 * high):
+                column = left + (k % 2) * 128
+                pg_out[row + k // 2, :, column : column + 128] = tiles[k]
+
+        plain = t * groups
+        if kind == "x":
+            row = half * (plain - 4 * ((t + 3) // 4)) + (1 - half) * (plain + 28)
+            store(0, 4, row)
+
+            @pl.when(t + 4 * (1 - half) > 0)
+            def _():
+                store(4, 8, half * (plain - 4) + (1 - half) * (plain + 28))
+        else:
+            row = half * (plain - 4 * ((t + 7) // 8)) + (1 - half) * (plain + 28)
+
+            @pl.when((t - 1) * (t - 1) + (1 - half) > 0)
+            def _():
+                store(0, 4, row)
 
     def spread_out(kind, i):
         t, rows = span(kind, i)
@@ -331,13 +346,13 @@
 
     for i in X_ORDER:
         back["x", i].wait_recv()
-    pack([gb[k // 2, :, (k % 2) * 128 : (k % 2) * 128 + 128] for k in range(8)], slot("y", core, yi))
+    pack([tile for k in range(4) for tile in unpack(gb.at[k], 2)], slot("y", core, yi))
     for i in Y_ORDER:
         spread_out("y", i)
     to_other("y", 0, yi)
     for i in Y_ORDER:
         back["y", i].wait_recv()
-    pack([ga[k // 2, :, (k % 2) * 128 : (k % 2) * 128 + 128] for k in range(16)], slot("x", core, xi))
+    pack([tile for k in range(8) for tile in unpack(ga.at[k], 2)], slot("x", core, xi))
     for i in X_ORDER:
         spread_out("x", i)
     to_other("x", 0, xi)
@@ -399,14 +414,14 @@
         pltpu.VMEM((3, 17, 16, 128), I16),
         pltpu.VMEM((7, 9, 16, 128), I16),
         pltpu.VMEM((7, 9, 16, 128), I16),
-        pltpu.VMEM((8, 16, 256), F32),
-        pltpu.VMEM((7, 16, 256), F32),
-        pltpu.VMEM((4, 16, 256), F32),
-        pltpu.VMEM((3, 16, 256), F32),
-        pltpu.VMEM((2, 4, 16, 256), F32),
-        pltpu.VMEM((2, 3, 16, 256), F32),
-        pltpu.VMEM((8, 16, 256), F32),
-        pltpu.VMEM((4, 16, 256), F32),
+        pltpu.VMEM((8, 3, 16, 128), I16),
+        pltpu.VMEM((7, 3, 16, 128), I16),
+        pltpu.VMEM((4, 3, 16, 128), I16),
+        pltpu.VMEM((3, 3, 16, 128), I16),
+        pltpu.VMEM((2, 4, 3, 16, 128), I16),
+        pltpu.VMEM((2, 3, 3, 16, 128), I16),
+        pltpu.VMEM((8, 3, 16, 128), I16),
+        pltpu.VMEM((4, 3, 16, 128), I16),
         pltpu.VMEM((2, 4, 17, 16, 128), I16),
         pltpu.VMEM((2, 8, 9, 16, 128), I16),
         pltpu.VMEM((4, 4 * GB, 128), F32),
@@ -424,7 +439,7 @@
         out_shape=(
             pltpu.VMEM((960, GB), F32),
             pltpu.VMEM((4, GB), F32),
-            pltpu.VMEM((64, 16, 512), F32),
+            pltpu.VMEM((60, 16, 512), F32),
         ),
         in_specs=[pl.BlockSpec(memory_space=pltpu.HBM)] * len(operands),
         out_specs=(pl.BlockSpec(memory_space=pltpu.VMEM),) * 3,
@@ -434,7 +449,7 @@
         ),
         name="fused",
     )(*operands)
-    return rows_t.T, new_state, pg[0:60].reshape(960, 512)
+    return rows_t.T, new_state, pg.reshape(960, 512)
 
 
 def solution(mesh):

time: 61.8 us -> 60 us (0.971)
  Pallas kernels: 57.9 us -> 56.4 us
    slice x1 -> x0, local copies, waits for them, and re-layouts: 1.55 us -> none  [on_device(): return (rows_t.T, new_state, pg[0:60].reshape(960, 512))]
    pallas_call x1, Pallas kernels: 57.9 us -> 56.4 us  [on_device(): pl.pallas_call(functools.partial(kernel, scale), out_shape=(pltpu.VMEM((9...]
    unnamed x2 -> x3, local copies, waits for them, and re-layouts: 1.54 us -> 2.81 us
where the time goes in v5:
time: 60 us; the launch traced here: 59.9 us
  Pallas kernels  56.4 us (94%)
  local copies, waits for them, and re-layouts  2.81 us (5%)
  between operations  0.64 us (1%)
    pallas_call x1, Pallas kernels, on_device(): pl.pallas_call(functools.partial(kernel, scale), out_shape=(pltpu.VMEM((9...  56.4 us
    unnamed x3, local copies, waits for them, and re-layouts  2.81 us

profile of v5, /device:TPU:1, one launch (start us, length us, event | category | flops | bytes accessed | tf_op | source)
XLA Modules:
  0.0 59.9 jit_solution(7835564697749818002)
XLA Ops:
  0.6 56.4 %fused.1 = (f32[960,256]{1,0:T(8,128)S(1)}, f32[4,256]{1,0:T(4,128)S(1)}, f32[60,16,512]{2,1,0:T(8,128)S(1)}) custom-call(bf16[256,4,512]{2,1,0:T(4,128)(2,1)} %bitcast.11, bf16[256,960]{1,0:T(8,128)(2,1)} %bitcast.13, bf16[960,512]{1,0:T(8,128)(2,1)} %proj.1, f32[960,256]{1,0:T(8,128)} %bitcast.12, f32[4,256]{1,0:T(4,128)} %state.1, ...), custom_call_target="tpu_custom_call" | custom-call | tf_op jit(solution)/shard_map/fused/pallas_call | solution.py:437
  57.1 0.9 %copy.13 = f32[256,960]{0,1:T(8,128)} copy(f32[256,960]{0,1:T(8,128)S(1)} %bitcast.10) | data formatting | bytes 1966080
  58.0 0.6 copy.14
  58.6 1.3 %copy.15 = f32[960,512]{1,0:T(8,128)} copy(f32[960,512]{1,0:T(8,128)S(1)} %bitcast.9) | data formatting | bytes 3932160

commit v6 on v5

--- a/solution.py
+++ b/solution.py
@@ -231,6 +231,29 @@
         copy.start()
         second["x", i] = copy
 
+    def to_owner(dy, dx, dc):
+        t = (lax.rem(yi + dy, NY) * NX + lax.rem(xi + dx, NX)) * 2 + lax.rem(core + dc, 2)
+        return remote(abuf.at[t], arecv.at[p], a_s, a_r, (g, t))
+
+    def send_bags(act, which):
+        if which == 0:
+
+            @pl.loop(0, 14)
+            def _(m):
+                act(to_owner(1 + m // 2, 0, lax.rem(m, 2)))
+
+            @pl.loop(1, 8)
+            def _(m):
+                act(to_owner(0, m // 2, lax.rem(m, 2)))
+        else:
+
+            @pl.loop(0, 42)
+            def _(m):
+                act(to_owner(1 + m // 6, 1 + lax.rem(m, 6) // 2, lax.rem(m, 2)))
+
+    send_bags(lambda copy: copy.start(), 0)
+    arecv[p] = abuf[p]
+
     def summed(terms):
         total = unpack(terms[0], 2)
         for term in terms[1:]:
@@ -254,17 +277,6 @@
             copies.append(remote(slot, slot, z2_s.at[n, i - 1], z2_r.at[n, i - 1], z_far(i)))
             copies[-1].start()
         return copies
-
-    def to_owner(i):
-        t = lax.rem(p + i, N_OWN)
-        return remote(abuf.at[t], arecv.at[p], a_s, a_r, (g, t))
-
-    def send_bags():
-        @pl.loop(1, N_OWN)
-        def _(i):
-            to_owner(i).start()
-
-        arecv[p] = abuf[p]
 
     z_copies = []
     waiting = []
@@ -275,7 +287,7 @@
         waiting.append(near(n, part))
         z_copies += waiting[-1]
         if n == 0:
-            send_bags()
+            send_bags(lambda copy: copy.start(), 1)
 
     for n in range(2):
         for copy in waiting[n]:
@@ -356,6 +368,13 @@
     for i in X_ORDER:
         spread_out("x", i)
     to_other("x", 0, xi)
+    put("y", core, yi)
+    put("x", core, xi)
+    for kind, i in (("x", 1), ("x", 3), ("x", 2), ("y", 1), ("y", 7), ("y", 2), ("y", 6), ("y", 3), ("y", 5), ("y", 4)):
+        last[kind, i].wait_recv()
+        t = lax.rem(xi - i + NX, NX) if kind == "x" else lax.rem(yi - i + NY, NY)
+        to_other(kind, i, t)
+        put(kind, core, t)
     pltpu.make_async_copy(arecv.at[pl.ds(0, N_OWN - 1)], arecv.at[pl.ds(0, N_OWN - 1)], a_r).wait()
     loads[5].wait()
     loads[6].wait()
@@ -375,13 +394,6 @@
         new = state_v[member : member + 1, :] + jnp.sum(grad * grad, axis=0, keepdims=True) * (1.0 / width)
         state_out[member : member + 1, :] = new
         rows_out[offset : offset + width, :] = emb_v[offset : offset + width, :] - grad * (LEARN / jnp.sqrt(new))
-    put("y", core, yi)
-    put("x", core, xi)
-    for kind, i in BOTH:
-        last[kind, i].wait_recv()
-        t = lax.rem(xi - i + NX, NX) if kind == "x" else lax.rem(yi - i + NY, NY)
-        to_other(kind, i, t)
-        put(kind, core, t)
     for kind, i in (("y", 0), ("x", 0)) + BOTH:
         hand[kind, i].wait_recv()
         t = lax.rem(xi - i + NX, NX) if kind == "x" else lax.rem(yi - i + NY, NY)
@@ -393,9 +405,8 @@
     for copy in z_copies:
         copy.wait_send()
 
-    @pl.loop(1, N_OWN)
-    def _(i):
-        to_owner(i).wait_send()
+    send_bags(lambda copy: copy.wait_send(), 0)
+    send_bags(lambda copy: copy.wait_send(), 1)
 
 
 def on_device(upstream, pooled, projection, embedding, row_state, lookups, bag_sizes):

time: 60 us -> 59.7 us (level)
  no operation moved by 1% of the time
where the time goes in v6:
time: 59.7 us; the launch traced here: 59.5 us
  Pallas kernels  56.1 us (94%)
  local copies, waits for them, and re-layouts  2.81 us (5%)
  between operations  0.64 us (1%)
    pallas_call x1, Pallas kernels, on_device(): pl.pallas_call(functools.partial(kernel, scale), out_shape=(pltpu.VMEM((9...  56.1 us
    unnamed x3, local copies, waits for them, and re-layouts  2.81 us

profile of v6, /device:TPU:1, one launch (start us, length us, event | category | flops | bytes accessed | tf_op | source)
XLA Modules:
  0.0 59.5 jit_solution(18343588507789642757)
XLA Ops:
  0.6 56.1 %fused.1 = (f32[960,256]{1,0:T(8,128)S(1)}, f32[4,256]{1,0:T(4,128)S(1)}, f32[60,16,512]{2,1,0:T(8,128)S(1)}) custom-call(bf16[256,4,512]{2,1,0:T(4,128)(2,1)} %bitcast.11, bf16[256,960]{1,0:T(8,128)(2,1)} %bitcast.13, bf16[960,512]{1,0:T(8,128)(2,1)} %proj.1, f32[960,256]{1,0:T(8,128)} %bitcast.12, f32[4,256]{1,0:T(4,128)} %state.1, ...), custom_call_target="tpu_custom_call" | custom-call | tf_op jit(solution)/shard_map/fused/pallas_call | solution.py:448
  56.7 0.9 %copy.13 = f32[256,960]{0,1:T(8,128)} copy(f32[256,960]{0,1:T(8,128)S(1)} %bitcast.10) | data formatting | bytes 1966080
  57.7 0.6 copy.14
  58.3 1.3 %copy.15 = f32[960,512]{1,0:T(8,128)} copy(f32[960,512]{1,0:T(8,128)S(1)} %bitcast.9) | data formatting | bytes 3932160
